TPU v7x, 256 devices: a whole 4x4x8 slice. The times are simulated.
256 devices in a mesh: dimer: 8 (over y_hi, x), grid: 32 (over z, y_lo, core).
Axes of the slice: x: 4, y: 4 (y_hi: 2, y_lo: 2; y = y_hi * 2 + y_lo), z: 8, core: 2. Of those that a mesh axis runs over, the one named last changes fastest.
Arguments:
- basis_values: bfloat16 [8, 40960, 1024], P('dimer', 'grid'), may hold values from -15 to 15
- aux_values: bfloat16 [8, 40960, 2048], P('dimer', 'grid'), may hold values from -6 to 6
- factors: bfloat16 [8, 512, 128], P('dimer', 'grid'), may hold values from -0.25 to 0.25
- frag_slot: int32 [8], replicated, may hold values from 0 to 7, each once
- dimer_pairs: int32 [8, 2], P('dimer'), may hold values from 0 to 7, as said below
- counts: int32 [8, 32], P('dimer', 'grid'), may hold values from 1 to 1280, 16384 in all within a row
- weights: float32 [8, 40960], P('dimer', 'grid'), may hold values from 0.000390625 to 0.0015625
- metric_inv: float32 [8, 2048, 2048], P('dimer', 'grid'), may hold values from -1 to 1, as said below
Outputs:
- frag_fock: float32 [8, 512, 512], P('dimer', 'grid')
- coupling: float32 [8, 512, 512], P('dimer', 'grid')
Inputs may be any that keep to these rules, and one draw needn't show every extreme that they name: `dimer_pairs`: each fragment is named by exactly two dimers, and the two fragments of a dimer differ. For each dimer the 32 counts sum to 16384 and the largest equals 1280. `metric_inv`: each matrix is symmetric.
All inputs are finite; a program needn't handle non-finite values. No bound on the sum of `counts` on one device may be relied on, other than what follows from the above.
Results may differ from a plain program's by a relative error of at most 0.0029.
Values may be sent and summed in bfloat16 or wider, within the bound.
A program may use at most 64 MiB of HBM per device.

v0:
```python
import jax
import jax.numpy as jnp
from jax import lax
from jax.sharding import PartitionSpec as P

exchange_coeff = 0.9847450218426964


def split_product(vector, matrix, vector_left):
    high_part = vector.astype(jnp.bfloat16)
    high_back = lax.optimization_barrier(high_part).astype(jnp.float32)
    low_part = (vector - high_back).astype(jnp.bfloat16)
    if vector_left:
        return jnp.dot(high_part, matrix, preferred_element_type=jnp.float32) + jnp.dot(
            low_part, matrix, preferred_element_type=jnp.float32
        )
    return jnp.dot(matrix, high_part, preferred_element_type=jnp.float32) + jnp.dot(
        matrix, low_part, preferred_element_type=jnp.float32
    )


def contract(left_side, right_side):
    numbers = (((0,), (0,)), ((), ()))
    return lax.dot_general(left_side, right_side, numbers, preferred_element_type=jnp.float32)


def shards(basis_values, aux_values, factors, frag_slot, dimer_pairs, counts, weights, metric_inv):
    highest = lax.Precision.HIGHEST
    basis_rows = basis_values[0]
    aux_block = aux_values[0]
    points = basis_rows.shape[0]
    frag_basis = basis_rows.shape[1] // 2
    live_count = counts[0, 0]
    position = lax.iota(jnp.int32, points)
    live_weight = jnp.where(position < live_count, weights[0], jnp.zeros((), jnp.float32))
    gathered = lax.all_gather(factors, "dimer", axis=0, tiled=True)
    frag_ids = lax.iota(jnp.int32, frag_slot.shape[0])
    wanted = jnp.sum(
        jnp.where(frag_ids[None, :] == dimer_pairs[0][:, None], frag_slot[None, :], 0), axis=1
    )
    selector = (frag_ids[None, :] == wanted[:, None]).astype(jnp.bfloat16)
    chosen = jnp.einsum(
        "as,srk->ark", selector, gathered, preferred_element_type=jnp.float32
    ).astype(jnp.bfloat16)
    dimer_factors = lax.all_gather(chosen, "grid", axis=1, tiled=True)
    orb_first = jnp.dot(
        basis_rows[:, :frag_basis], dimer_factors[0], preferred_element_type=jnp.float32
    )
    orb_second = jnp.dot(
        basis_rows[:, frag_basis:], dimer_factors[1], preferred_element_type=jnp.float32
    )
    density = (
        jnp.sum(orb_first * orb_first, axis=1) + jnp.sum(orb_second * orb_second, axis=1)
    ) / (2.0 * dimer_factors.shape[2])
    exchange = -exchange_coeff * jnp.cbrt(density)
    weighted_density = live_weight * density
    fitted = lax.psum(split_product(weighted_density, aux_block, True), "grid")
    coef_rows = jnp.dot(metric_inv[0], fitted, precision=highest)
    coefficients = lax.all_gather(coef_rows, "grid", axis=0, tiled=True)
    coulomb = split_product(coefficients, aux_block, False)
    potential_total, weight_sum = lax.psum(
        (jnp.sum(live_weight * (coulomb + exchange)), jnp.sum(live_weight)), "grid"
    )
    average = potential_total / weight_sum
    potential = live_weight * (coulomb + exchange - average)
    weighted_basis = (basis_rows * potential[:, None]).astype(jnp.bfloat16)
    half_rows = frag_basis // lax.axis_size("grid")
    groups = 2 * half_rows * lax.axis_size("grid") // (2 * half_rows)
    first_index = jnp.int32(0) // 2
    left_first = lax.dynamic_slice_in_dim(
        weighted_basis, first_index, groups * half_rows, 1
    ).reshape(points, groups, half_rows)
    left_second = lax.dynamic_slice_in_dim(
        weighted_basis, frag_basis, groups * half_rows, 1
    ).reshape(points, groups, half_rows)
    left_side = jnp.concatenate([left_first, left_second], axis=2).reshape(
        points, 2 * half_rows * lax.axis_size("grid")
    )
    shares = lax.psum_scatter(
        contract(left_side, basis_rows), "grid", scatter_dimension=0, tiled=True
    )
    own_first = shares[:half_rows, :frag_basis]
    own_cross = shares[:half_rows, frag_basis:]
    own_second = shares[half_rows:, frag_basis:]
    is_first = (frag_ids == dimer_pairs[0, 0])[:, None, None]
    is_second = (frag_ids == dimer_pairs[0, 1])[:, None, None]
    fock_terms = jnp.where(is_first, own_first[None], jnp.zeros((), jnp.float32)) + jnp.where(
        is_second, own_second[None], jnp.zeros((), jnp.float32)
    )
    frag_fock = lax.psum_scatter(fock_terms, "dimer", scatter_dimension=0, tiled=True)
    return (frag_fock, own_cross[None])


def solution(mesh):
    placed = (
        P("dimer", "grid", None),
        P("dimer", "grid", None),
        P("dimer", "grid", None),
        P(),
        P("dimer", None),
        P("dimer", "grid"),
        P("dimer", "grid"),
        P("dimer", "grid", None),
    )
    return jax.shard_map(
        shards,
        mesh=mesh,
        in_specs=placed,
        out_specs=(P("dimer", "grid", None), P("dimer", "grid", None)),
        check_vma=False,
    )
```

profile of v0, /device:TPU:24, one launch (start us, length us, event | category | flops | bytes accessed | tf_op | source)
XLA Modules:
  0.0 474.6 jit_solution(4176700981948331173)
XLA Ops:
  8.0 3.0 copy.17
  11.0 34.1 %all_gather.9 = bf16[8,16,128]{2,1,0:T(8,128)(2,1)S(1)} all-gather(bf16[1,16,128]{2,1,0:T(8,128)(2,1)S(1)} %copy-done.4), channel_id=1, replica_groups=mesh['dimer'=8,'grid'=32] {'dimer'}, dimensions={0}, use_global_device_ids=true | all-gather | bytes 36864 | tf_op jit(solution)/shard_map/all_gather | solution.py:36
  45.1 0.2 fusion.39
  45.2 0.2 convolution_convert_fusion
  45.4 35.0 %all_gather.10 = bf16[2,512,128]{2,0,1:T(2,128)(2,1)S(1)} all-gather(bf16[2,16,128]{2,0,1:T(2,128)(2,1)S(1)} %convolution_convert_fusion), channel_id=1, replica_groups=mesh['dimer'=8,'grid'=32] {'grid'}, dimensions={1}, use_global_device_ids=true | all-gather | bytes 270336 | tf_op jit(solution)/shard_map/all_gather | solution.py:45
  80.4 0.4 fusion.44
  80.8 0.4 fusion.12
  81.2 0.4 fusion.15
  81.6 3.4 fusion.4
  85.1 0.6 copy-done.1
  85.7 0.8 fusion.6
  86.5 53.3 %psum.21 = f32[2048]{0:T(1024)S(1)} all-reduce(f32[2048]{0:T(1024)S(1)} %add.37), channel_id=1, replica_groups=mesh['dimer'=8,'grid'=32] {'grid'}, use_global_device_ids=true, to_apply=%region_3.4 | all-reduce | flops 2048 | bytes 16384 | tf_op jit(solution)/shard_map/psum | solution.py:57
  139.8 0.5 convolution_bitcast_fusion
  140.3 0.6 dynamic-slice
  141.6 0.3 dynamic-update-slice
  141.8 54.0 %all-reduce = f32[2048]{0:T(1024)S(1)} all-reduce(f32[2048]{0:T(1024)S(1)} %dynamic-update-slice), channel_id=1, replica_groups=mesh['dimer'=8,'grid'=32] {'grid'}, use_global_device_ids=true, to_apply=%add | all-reduce | flops 2048 | bytes 16384
  195.9 4.0 fusion.21
  199.9 4.0 fusion.18
  203.8 0.7 fusion.27
  204.5 53.6 %all-reduce.1 = (f32[]{:T(128)}, f32[]{:T(128)}) all-reduce(f32[]{:T(128)} %get-tuple-element.3, f32[]{:T(128)} %get-tuple-element.2), channel_id=1, replica_groups=mesh['dimer'=8,'grid'=32] {'grid'}, use_global_device_ids=true, to_apply=%region_5.6 | all-reduce | flops 2 | bytes 16 | tf_op jit(solution)/shard_map/psum | solution.py:61
  259.5 0.5 multiply_convert_fusion
  260.0 0.2 fusion.43
  260.2 0.3 pad_maximum_fusion
  260.5 1.4 copy-done.2
  261.9 4.4 fusion.8
  266.3 0.0 reduce-scatter.5.cloned.1.call-start
  266.4 0.6 fusion.45
  266.9 1.3 iota_compare_fusion.1
  268.3 118.6 %reduce-scatter.3.cloned.1.call-done = f32[32,1024]{1,0:T(8,128)} async-done(((f32[1024,1024]{1,0:T(8,128)}), f32[32,1024]{1,0:T(8,128)}) %reduce-scatter.3.cloned.1.call-update) | async-done | bytes 131088 | tf_op jit(solution)/shard_map/reduce_scatter | solution.py:79
  386.8 1.4 slice_bitcast_fusion
  388.2 0.8 select_add_fusion
  389.0 78.7 %reduce-scatter.5.cloned.1.call-done = f32[1,16,512]{2,1,0:T(8,128)} async-done(((f32[8,16,512]{2,1,0:T(8,128)}), f32[1,16,512]{2,1,0:T(8,128)}) %reduce-scatter.5.cloned.1.call-update) | async-done | bytes 32784 | tf_op jit(solution)/shard_map/reduce_scatter | solution.py:90
  (28 shorter events, 0.2 us)
Async XLA Ops:
  7.2 132.6 %copy-start = (f32[1,64,2048]{2,1,0:T(8,128)S(1)}, f32[1,64,2048]{2,1,0:T(8,128)}, u32[]{:S(2)}) copy-start(f32[1,64,2048]{2,1,0:T(8,128)} %param.15) | copy-start | bytes 1572868
  7.2 379.6 %reduce-scatter.3.cloned.1.call-start = ((), (), s32[]{:S(2)}) async-start(), calls=%async_computation.2 | async-start | bytes 4325376 | tf_op jit(solution)/shard_map/reduce_scatter | solution.py:79
  7.9 3.0 copy-start.4
  7.9 37.1 %copy-start.5 = (s32[1,2]{1,0:T(1,128)S(1)}, s32[1,2]{1,0:T(1,128)}, u32[]{:S(2)}) copy-start(s32[1,2]{1,0:T(1,128)} %param.12) | copy-start | bytes 28
  7.9 37.1 %copy-start.6 = (s32[8]{0:T(128)S(1)}, s32[8]{0:T(128)}, u32[]{:S(2)}) copy-start(s32[8]{0:T(128)} %param.11) | copy-start | bytes 100
  11.0 70.6 %copy-start.3 = (f32[1,1280]{1,0:T(1,128)S(1)}, f32[1,1280]{1,0:T(1,128)}, u32[]{:S(2)}) copy-start(f32[1,1280]{1,0:T(1,128)} %param.14) | copy-start | bytes 15364
  81.6 4.0 copy-start.1
  85.7 54.6 %copy-start.7 = (u32[256]{0:T(256)S(1)}, u32[256]{0:T(256)}, u32[]{:S(2)}) copy-start(u32[256]{0:T(256)} %constant.35) | copy-start | bytes 3076
  260.1 1.7 copy-start.2
  266.3 201.4 %reduce-scatter.5.cloned.1.call-start = ((), (), s32[]{:S(2)}) async-start(), calls=%async_computation.3 | async-start | bytes 294912 | tf_op jit(solution)/shard_map/reduce_scatter | solution.py:90
Sparse Core Ops, SparseCore 0:
  266.4 120.3 reduce-scatter.2
  391.2 76.4 reduce-scatter.4
where the time goes:
time: 476 us; the launch traced here: 475 us
  blocking collectives  230 us (48%)
  waiting for transfers between devices  197 us (41%)
  matrix products  18 us (4%)
  between operations  16.9 us (4%)
  local copies, waits for them, and re-layouts  8.46 us (2%)
    reduce_scatter x1, waiting for transfers between devices, shards(): lax.psum_scatter(contract(left_side, basis_rows), 'grid', scatter_dimensi...  119 us
    reduce_scatter x1, waiting for transfers between devices, shards(): lax.psum_scatter(fock_terms, 'dimer', scatter_dimension=0, tiled=True)  78.7 us
    unnamed x1, blocking collectives  54 us
    psum x1, blocking collectives, shards(): lax.psum((jnp.sum(live_weight * (coulomb + exchange)), jnp.sum(live_weigh...  53.6 us
    psum x1, blocking collectives, shards(): fitted = lax.psum(split_product(weighted_density, aux_block, True), 'grid')  53.3 us
    all_gather x1, blocking collectives, shards(): dimer_factors = lax.all_gather(chosen, 'grid', axis=1, tiled=True)  35 us
    all_gather x1, blocking collectives, shards(): gathered = lax.all_gather(factors, 'dimer', axis=0, tiled=True)  34.1 us
  transfers between devices with their start and end apart: 2, of which 2 were waited for; matrix products, arithmetic and copies ran while one was open for 0% of the time, Pallas kernels for 0%

commit v1 on v0

v1 whole, which is shorter than its diff:
```python
import functools

import jax
import jax.numpy as jnp
from jax import lax
from jax.experimental import pallas as pl
from jax.experimental.pallas import tpu as pltpu
from jax.sharding import PartitionSpec as P

EXCHANGE_COEFF = 0.9847450218426964
GRID = 32
DIMERS = 8
CHIPS = 16
PTS = 1280
FB = 512
OCC = 128
AUX = 2048
F32 = jnp.float32
BF16 = jnp.bfloat16
MESH = pl.DeviceIdType.MESH


def wait_bytes(ref, sem):
    pltpu.make_async_copy(ref, ref, sem).wait()


def remote(src, dst, send_sem, recv_sem, axis, index):
    copy = pltpu.make_async_remote_copy(
        src_ref=src,
        dst_ref=dst,
        send_sem=send_sem,
        recv_sem=recv_sem,
        device_id={axis: index},
        device_id_type=MESH,
    )
    copy.start()


def hi_lo_rows(row):
    high = row.astype(BF16)
    low = (row - high.astype(F32)).astype(BF16)
    which = lax.broadcasted_iota(jnp.int32, (16, row.shape[1]), 0)
    zero = jnp.zeros((16, row.shape[1]), F32)
    high, low = high.astype(F32), low.astype(F32)
    return jnp.where(which == 0, high, jnp.where(which == 1, low, zero)).astype(BF16)


def cube_root(x):
    safe = jnp.where(x > 0, x, 1.0)
    y = jnp.exp(jnp.log(safe) * (1.0 / 3.0))
    y = y - (y - safe / (y * y)) * (1.0 / 3.0)
    return jnp.where(x > 0, y, 0.0)


def dot(a, b):
    return jnp.dot(a, b, preferred_element_type=F32)


def kernel(
    basis_hbm, aux_hbm, fac_ref, slot_ref, pairs_ref, counts_ref, weights_ref, metric_hbm,
    frag_out, coup_out,
    b, aux, bt, wt, mbuf, facbuf, facsend, facall,
    ssend, srecv, fsend, frecv, csend, crecv,
    acc, core_send, core_recv, y_send, y_recv, z_send, z_recv, d_send, d_recv,
    local_sem, fa_sem, fb_sem, fc_sem, m_sem, s_sem, f_sem, c_sem,
    core_sem, y_sem, z_sem, d_sem,
):
    d = lax.axis_index("dimer")
    g = lax.axis_index("grid")
    core = lax.rem(g, 2)
    chip = g // 2
    y = lax.rem(chip, 2)
    z = chip // 2
    other_core = g + 1 - 2 * core
    other_y = g + 2 - 4 * y

    load_b = pltpu.make_async_copy(basis_hbm.at[0], b, local_sem.at[0])
    load_aux = pltpu.make_async_copy(aux_hbm.at[0], aux, local_sem.at[1])
    load_m = pltpu.make_async_copy(metric_hbm.at[0], mbuf.at[core], local_sem.at[2])
    load_b.start()
    load_aux.start()
    load_m.start()

    barrier = pltpu.get_barrier_semaphore()
    for k in range(1, GRID):
        pl.semaphore_signal(
            barrier, inc=1, device_id={"grid": lax.rem(g + k, GRID)}, device_id_type=MESH
        )
    for k in range(1, DIMERS):
        pl.semaphore_signal(
            barrier, inc=1, device_id={"dimer": lax.rem(d + k, DIMERS)}, device_id_type=MESH
        )
    pl.semaphore_wait(barrier, GRID - 1 + DIMERS - 1)

    for k in range(1, DIMERS):
        remote(
            fac_ref.at[0], facbuf.at[d], fa_sem.at[0], fa_sem.at[1],
            "dimer", lax.rem(d + k, DIMERS),
        )
    facbuf[d] = fac_ref[0]
    remote(metric_hbm.at[0], mbuf.at[core], m_sem.at[0], m_sem.at[1], "grid", other_core)

    load_b.wait()
    for block in range(8):
        turned = b[:, block * 128:(block + 1) * 128].T
        for part in range(8):
            group = block * 8 + part
            half, owner = group // 32, group % 32
            place = half * 32 + (owner % 2) * 16 + ((owner // 2) % 2) * 8 + owner // 4
            bt[place * 16:(place + 1) * 16, :] = turned[part * 16:(part + 1) * 16, :]

    first, second = pairs_ref[0, 0], pairs_ref[0, 1]
    place = core * 256 + y * 128 + z * 16
    rows = pl.ds(pl.multiple_of(place, 16), 16)
    wait_bytes(facbuf.at[pl.ds(0, DIMERS - 1)], fa_sem.at[1])
    facsend[0] = facbuf[slot_ref[first]]
    facsend[1] = facbuf[slot_ref[second]]
    facall[:, rows, :] = facsend[...]
    for k in range(1, CHIPS):
        remote(
            facsend, facall.at[:, rows, :], fb_sem.at[0], fb_sem.at[1],
            "grid", 2 * lax.rem(chip + k, CHIPS) + core,
        )

    position = lax.broadcasted_iota(jnp.int32, (1, PTS), 1)
    lw = jnp.where(position < counts_ref[0, 0], weights_ref[...], 0.0)
    load_aux.wait()
    sums = dot(hi_lo_rows(lw), aux[...])
    sums = sums[0:1, :] + sums[1:2, :]
    for k in range(CHIPS):
        ssend[k] = sums[:, k * 128:(k + 1) * 128]
    srecv[g] = ssend[chip]
    for k in range(1, GRID):
        to = lax.rem(g + k, GRID)
        remote(ssend.at[to // 2], srecv.at[g], s_sem.at[0], s_sem.at[1], "grid", to)

    wait_bytes(facall.at[:, pl.ds(0, 240), :], fb_sem.at[1])
    own_half = pl.ds(pl.multiple_of(core * 256, 256), 256)
    remote(
        facall.at[:, own_half, :], facall.at[:, own_half, :], fc_sem.at[0], fc_sem.at[1],
        "grid", other_core,
    )
    wait_bytes(facall.at[:, pl.ds(0, 256), :], fc_sem.at[1])

    turn = (((0,), (0,)), ((), ()))
    density = jnp.zeros((1, PTS), F32)
    for half in range(2):
        orbitals = lax.dot_general(
            facall[half], bt[half * FB:(half + 1) * FB, :], turn, preferred_element_type=F32
        )
        density += jnp.sum(orbitals * orbitals, axis=0, keepdims=True)
    density = density * (1.0 / (2.0 * OCC))
    exchange = -EXCHANGE_COEFF * cube_root(density)

    fitted = dot(hi_lo_rows(lw * density), aux[...])
    fsend[...] = fitted[0:1, :] + fitted[1:2, :]
    frecv[chip] = fsend[...]
    for k in range(1, CHIPS):
        remote(
            fsend, frecv.at[chip], f_sem.at[0], f_sem.at[1],
            "grid", 2 * lax.rem(chip + k, CHIPS) + core,
        )
    local_exchange = jnp.sum(lw * exchange, axis=1, keepdims=True)
    local_weight = jnp.sum(lw, axis=1, keepdims=True)
    wait_bytes(srecv.at[pl.ds(0, GRID - 1)], s_sem.at[1])
    s_total = jnp.sum(srecv[...], axis=0)
    load_m.wait()
    wait_bytes(mbuf.at[0], m_sem.at[1])
    wait_bytes(frecv.at[pl.ds(0, CHIPS - 1)], f_sem.at[1])
    own_fitted = jnp.sum(frecv[...], axis=0)

    rows_m = jnp.concatenate([mbuf[0], mbuf[1]], axis=0)
    terms = rows_m[:, 0:128] * own_fitted[:, 0:128]
    for k in range(1, CHIPS):
        cols = slice(k * 128, (k + 1) * 128)
        terms += rows_m[:, cols] * own_fitted[:, cols]
    coef_part = jnp.sum(terms.T, axis=0, keepdims=True)
    total_part = jnp.sum(coef_part * s_total, axis=1, keepdims=True) + local_exchange
    lane = lax.broadcasted_iota(jnp.int32, (1, 128), 1)
    csend[0:1, :] = coef_part
    csend[1:2, :] = jnp.where(lane == 0, total_part, jnp.where(lane == 1, local_weight, 0.0))
    crecv[g] = csend[...]
    for k in range(1, GRID):
        remote(
            csend, crecv.at[g], c_sem.at[0], c_sem.at[1], "grid", lax.rem(g + k, GRID)
        )
    wait_bytes(crecv.at[pl.ds(0, GRID - 1)], c_sem.at[1])

    totals = jnp.sum(crecv[...], axis=0)[1:2, :]
    average = totals[:, 0:1] / totals[:, 1:2]
    coefficients = jnp.concatenate(
        [crecv[2 * k, 0:1, :] + crecv[2 * k + 1, 0:1, :] for k in range(CHIPS)], axis=1
    )
    numbers = (((1,), (1,)), ((), ()))
    coulomb = lax.dot_general(
        hi_lo_rows(coefficients), aux[...], numbers, preferred_element_type=F32
    )
    coulomb = coulomb[0:1, :] + coulomb[1:2, :]
    potential = lw * (coulomb + exchange - average)
    wt[...] = (bt[...].astype(F32) * potential).astype(BF16)

    blocks = ((0, 0), (1, 1), (0, 1))

    def product(block, of_core):
        half, column = blocks[block]
        at = pl.ds(pl.multiple_of(half * FB + of_core * 256, 256), 256)
        return dot(wt[at, :], b[:, column * FB:(column + 1) * FB])

    def core_stage(block):
        core_send[block] = product(block, 1 - core)
        remote(
            core_send.at[block], core_recv.at[block],
            core_sem.at[0, block], core_sem.at[1, block], "grid", other_core,
        )
        acc[block] = product(block, core)

    def y_stage(block):
        wait_bytes(core_recv.at[block], core_sem.at[1, block])
        there = pl.ds(pl.multiple_of((1 - y) * 128, 128), 128)
        y_send[block] = (acc[block, there, :] + core_recv[block, there, :]).astype(BF16)
        remote(
            y_send.at[block], y_recv.at[block],
            y_sem.at[0, block], y_sem.at[1, block], "grid", other_y,
        )

    def z_stage(block):
        here = pl.ds(pl.multiple_of(y * 128, 128), 128)
        own = acc[block, here, :] + core_recv[block, here, :]
        wait_bytes(y_recv.at[block], y_sem.at[1, block])
        own = own + y_recv[block].astype(F32)
        acc[block, pl.ds(0, 128), :] = own
        z_send[block] = own.astype(BF16)
        for k in range(1, 8):
            to = lax.rem(z + k, 8)
            at = pl.ds(pl.multiple_of(to * 16, 16), 16)
            remote(
                z_send.at[block, at, :], z_recv.at[block, k - 1],
                z_sem.at[0, block], z_sem.at[1, block], "grid", to * 4 + y * 2 + core,
            )

    def shares(block):
        at = pl.ds(pl.multiple_of(z * 16, 16), 16)
        own = acc[block, at, :]
        wait_bytes(z_recv.at[block], z_sem.at[1, block])
        for k in range(7):
            own = own + z_recv[block, k].astype(F32)
        return own

    core_stage(0)
    core_stage(1)
    y_stage(0)
    core_stage(2)
    y_stage(1)
    y_stage(2)
    z_stage(0)
    z_stage(1)
    z_stage(2)
    own_first = shares(0)
    own_second = shares(1)

    def for_fragment(index):
        return jnp.where(first == index, own_first, 0.0) + jnp.where(
            second == index, own_second, 0.0
        )

    for k in range(1, DIMERS):
        to = lax.rem(d + k, DIMERS)
        d_send[k - 1] = for_fragment(to)
        remote(
            d_send.at[k - 1], d_recv.at[k - 1], d_sem.at[0], d_sem.at[1], "dimer", to
        )
    own = for_fragment(d)
    coup_out[0] = shares(2)
    wait_bytes(d_recv, d_sem.at[1])
    for k in range(DIMERS - 1):
        own = own + d_recv[k]
    frag_out[0] = own

    wait_bytes(facbuf.at[pl.ds(0, DIMERS - 1)], fa_sem.at[0])
    wait_bytes(mbuf.at[0], m_sem.at[0])
    wait_bytes(facall.at[:, pl.ds(0, 240), :], fb_sem.at[0])
    wait_bytes(facall.at[:, pl.ds(0, 256), :], fc_sem.at[0])
    wait_bytes(srecv.at[pl.ds(0, GRID - 1)], s_sem.at[0])
    wait_bytes(frecv.at[pl.ds(0, CHIPS - 1)], f_sem.at[0])
    wait_bytes(crecv.at[pl.ds(0, GRID - 1)], c_sem.at[0])
    for block in range(3):
        wait_bytes(core_recv.at[block], core_sem.at[0, block])
        wait_bytes(y_recv.at[block], y_sem.at[0, block])
        wait_bytes(z_recv.at[block], z_sem.at[0, block])
    wait_bytes(d_recv, d_sem.at[0])


def shards(basis_values, aux_values, factors, frag_slot, dimer_pairs, counts, weights, metric_inv):
    vmem = pl.BlockSpec(memory_space=pltpu.VMEM)
    smem = pl.BlockSpec(memory_space=pltpu.SMEM)
    hbm = pl.BlockSpec(memory_space=pl.ANY)
    dma = pltpu.SemaphoreType.DMA
    share = jax.ShapeDtypeStruct((1, FB // GRID, FB), F32)
    return pl.pallas_call(
        kernel,
        name="fock",
        out_shape=(share, share),
        in_specs=[hbm, hbm, vmem, smem, smem, smem, vmem, hbm],
        out_specs=(vmem, vmem),
        scratch_shapes=[
            pltpu.VMEM((PTS, 2 * FB), BF16),
            pltpu.VMEM((PTS, AUX), BF16),
            pltpu.VMEM((2 * FB, PTS), BF16),
            pltpu.VMEM((2 * FB, PTS), BF16),
            pltpu.VMEM((2, AUX // GRID, AUX), F32),
            pltpu.VMEM((DIMERS, FB // GRID, OCC), BF16),
            pltpu.VMEM((2, FB // GRID, OCC), BF16),
            pltpu.VMEM((2, FB, OCC), BF16),
            pltpu.VMEM((CHIPS, 1, 128), F32),
            pltpu.VMEM((GRID, 1, 128), F32),
            pltpu.VMEM((1, AUX), F32),
            pltpu.VMEM((CHIPS, 1, AUX), F32),
            pltpu.VMEM((2, 128), F32),
            pltpu.VMEM((GRID, 2, 128), F32),
            pltpu.VMEM((3, 256, FB), F32),
            pltpu.VMEM((3, 256, FB), F32),
            pltpu.VMEM((3, 256, FB), F32),
            pltpu.VMEM((3, 128, FB), BF16),
            pltpu.VMEM((3, 128, FB), BF16),
            pltpu.VMEM((3, 128, FB), BF16),
            pltpu.VMEM((3, 7, 16, FB), BF16),
            pltpu.VMEM((DIMERS - 1, 16, FB), F32),
            pltpu.VMEM((DIMERS - 1, 16, FB), F32),
            dma((3,)), dma((2,)), dma((2,)), dma((2,)), dma((2,)), dma((2,)), dma((2,)), dma((2,)),
            dma((2, 3)), dma((2, 3)), dma((2, 3)), dma((2,)),
        ],
        compiler_params=pltpu.CompilerParams(
            collective_id=0, has_side_effects=True, vmem_limit_bytes=60 * 1024 * 1024
        ),
        cost_estimate=pl.CostEstimate(
            flops=2 * PTS * (2 * FB * OCC + 3 * AUX + 3 * FB * FB),
            bytes_accessed=2 * PTS * (2 * FB + AUX) + 4 * AUX * AUX // GRID,
            transcendentals=2 * PTS,
        ),
    )(basis_values, aux_values, factors, frag_slot, dimer_pairs, counts, weights, metric_inv)


def solution(mesh):
    placed = (
        P("dimer", "grid", None),
        P("dimer", "grid", None),
        P("dimer", "grid", None),
        P(),
        P("dimer", None),
        P("dimer", "grid"),
        P("dimer", "grid"),
        P("dimer", "grid", None),
    )
    return jax.shard_map(
        shards,
        mesh=mesh,
        in_specs=placed,
        out_specs=(P("dimer", "grid", None), P("dimer", "grid", None)),
        check_vma=False,
    )
```

time: 476 us -> 63.6 us (0.13)
  blocking collectives: 230 us -> 0 us
  waiting for transfers between devices: 197 us -> 0 us
  Pallas kernels: 0 us -> 59.3 us
  matrix products: 18 us -> 0 us
  between operations: 16.9 us -> 1.29 us
  local copies, waits for them, and re-layouts: 8.46 us -> 2.75 us
    reduce_scatter x2 -> x0, waiting for transfers between devices: 197 us -> none  [the longest x1 119 us: shards(): lax.psum_scatter(contract(left_side, basis_rows), 'grid', scatter_dimensi...]
    psum x2 -> x0, blocking collectives: 107 us -> none  [the longest x1 53.6 us: shards(): lax.psum((jnp.sum(live_weight * (coulomb + exchange)), jnp.sum(live_weigh...]
    all_gather x2 -> x0, blocking collectives: 69 us -> none  [the longest x1 35 us: shards(): dimer_factors = lax.all_gather(chosen, 'grid', axis=1, tiled=True)]
    pallas_call x0 -> x1, Pallas kernels: none -> 59.3 us  [shards(): pl.pallas_call(kernel, name='fock', out_shape=(share, share), in_specs=[h...]
    unnamed x1 -> x0, blocking collectives: 54 us -> none
    dot_general x9 -> x0, matrix products: 18 us -> none  [the longest x1 4.41 us: contract(): lax.dot_general(left_side, right_side, numbers, preferred_element_type=jn...]
  transfers between devices with their start and end apart: 2 -> 0, of which waited for: 2 -> 0; matrix products, arithmetic and copies ran while one was open for 0% -> 0% of each run, Pallas kernels for 0% -> 0%
where the time goes in v1:
time: 63.6 us; the launch traced here: 63.4 us
  Pallas kernels  59.3 us (93%)
  local copies, waits for them, and re-layouts  2.75 us (4%)
  between operations  1.29 us (2%)
    pallas_call x1, Pallas kernels, shards(): pl.pallas_call(kernel, name='fock', out_shape=(share, share), in_specs=[h...  59.3 us
    unnamed x2, local copies, waits for them, and re-layouts  2.75 us

profile of v1, /device:TPU:24, one launch (start us, length us, event | category | flops | bytes accessed | tf_op | source)
XLA Modules:
  0.0 63.4 jit_solution(9992020828553998618)
XLA Ops:
  1.3 59.3 %fock.1 = (f32[1,16,512]{2,1,0:T(8,128)}, f32[1,16,512]{2,1,0:T(8,128)}) custom-call(bf16[1,1280,1024]{2,1,0:T(8,128)(2,1)} %basis_hbm.1, bf16[1,1280,2048]{2,1,0:T(8,128)(2,1)} %aux_hbm.1, bf16[1,16,128]{2,1,0:T(8,128)(2,1)} %fac_ref.1, s32[8]{0:T(128)} %slot_ref.1, s32[1,2]{1,0:T(1,128)} %pairs_ref.1, s32[1,1]{1,0:T(1,128)S(6)} %copy.12.counts_ref, ...), custom_call_target="tpu_custom_call" | custom-call | flops 2364538880 | bytes 8388608 | tf_op jit(solution)/shard_map/fock/pallas_call | solution.py:299
  60.6 1.4 %copy.13 = f32[1,16,512]{2,1,0:T(8,128)} copy(f32[1,16,512]{2,1,0:T(8,128)} %get-tuple-element.4) | data formatting | bytes 65536
  62.0 1.4 %copy.14 = f32[1,16,512]{2,1,0:T(8,128)} copy(f32[1,16,512]{2,1,0:T(8,128)} %get-tuple-element.5) | data formatting | bytes 65536

commit v2 on v1

v2 whole, which is shorter than its diff:
```python
import functools

import jax
import jax.numpy as jnp
from jax import lax
from jax.experimental import pallas as pl
from jax.experimental.pallas import tpu as pltpu
from jax.sharding import PartitionSpec as P

EXCHANGE_COEFF = 0.9847450218426964
GRID = 32
DIMERS = 8
CHIPS = 16
FAR_GRID = sorted(range(1, 32), key=lambda k: -min(k, 32 - k))
FAR_CHIPS = sorted(range(1, 16), key=lambda k: -min(k, 16 - k))
FAR_Z = sorted(range(1, 8), key=lambda k: -min(k, 8 - k))
FAR_DIMERS = (2, 6, 4, 1, 3, 5, 7)
NC = 256
CHUNKS = (
    (1, 768, "z"), (0, 0, "y"), (0, 256, "y"), (1, 512, "y"), (0, 512, "y"), (0, 768, "y"),
)
SCHEDULE = (
    "o0 w0 o1 w1", "o2 s0 w2 s1", "o3 w3 s2 o4", "w4 s3 o5 w5", "t1 s4 t2 s5",
    "t3 t0 t4 t5",
)
PTS = 1280
FB = 512
OCC = 128
AUX = 2048
F32 = jnp.float32
BF16 = jnp.bfloat16
MESH = pl.DeviceIdType.MESH


def wait_bytes(ref, sem):
    pltpu.make_async_copy(ref, ref, sem).wait()


def remote(src, dst, send_sem, recv_sem, axis, index):
    copy = pltpu.make_async_remote_copy(
        src_ref=src,
        dst_ref=dst,
        send_sem=send_sem,
        recv_sem=recv_sem,
        device_id={axis: index},
        device_id_type=MESH,
    )
    copy.start()


def hi_lo_rows(row):
    high = row.astype(BF16)
    low = (row - high.astype(F32)).astype(BF16)
    which = lax.broadcasted_iota(jnp.int32, (16, row.shape[1]), 0)
    zero = jnp.zeros((16, row.shape[1]), F32)
    high, low = high.astype(F32), low.astype(F32)
    return jnp.where(which == 0, high, jnp.where(which == 1, low, zero)).astype(BF16)


def cube_root(x):
    safe = jnp.where(x > 0, x, 1.0)
    y = jnp.exp(jnp.log(safe) * (1.0 / 3.0))
    y = y - (y - safe / (y * y)) * (1.0 / 3.0)
    return jnp.where(x > 0, y, 0.0)


def dot(a, b):
    return jnp.dot(a, b, preferred_element_type=F32)


def kernel(
    basis_hbm, aux_hbm, fac_ref, slot_ref, pairs_ref, counts_ref, weights_ref, metric_hbm,
    out,
    b, aux, bt, auxt, wt, mbuf, facbuf, facsend, facall,
    ssend, srecv, fsend, frecv, csend, crecv,
    acc, core_send, core_recv, y_send, y_recv, z_send, z_recv,
    w_send, w_recv, v_send, v_recv, d_send, d_recv,
    local_sem, fa_sem, fb_sem, fc_sem, m_sem, s_sem, f_sem, c_sem,
    core_sem, y_sem, z_sem, d_sem,
):
    d = lax.axis_index("dimer")
    g = lax.axis_index("grid")
    core = lax.rem(g, 2)
    chip = g // 2
    y = lax.rem(chip, 2)
    z = chip // 2
    other_core = g + 1 - 2 * core
    other_y = g + 2 - 4 * y

    load_b = pltpu.make_async_copy(basis_hbm.at[0], b, local_sem.at[0])
    load_aux = pltpu.make_async_copy(aux_hbm.at[0], aux, local_sem.at[1])
    load_m = pltpu.make_async_copy(metric_hbm.at[0], mbuf.at[core], local_sem.at[2])
    load_b.start()
    load_aux.start()
    load_m.start()

    barrier = pltpu.get_barrier_semaphore()
    for k in FAR_GRID:
        pl.semaphore_signal(
            barrier, inc=1, device_id={"grid": lax.rem(g + k, GRID)}, device_id_type=MESH
        )
    for k in FAR_DIMERS:
        pl.semaphore_signal(
            barrier, inc=1, device_id={"dimer": lax.rem(d + k, DIMERS)}, device_id_type=MESH
        )
    pl.semaphore_wait(barrier, GRID - 1 + DIMERS - 1)

    for k in FAR_DIMERS:
        remote(
            fac_ref.at[0], facbuf.at[d], fa_sem.at[0], fa_sem.at[1],
            "dimer", lax.rem(d + k, DIMERS),
        )
    facbuf[d] = fac_ref[0]
    remote(metric_hbm.at[0], mbuf.at[core], m_sem.at[0], m_sem.at[1], "grid", other_core)

    position = lax.broadcasted_iota(jnp.int32, (1, PTS), 1)
    lw = jnp.where(position < counts_ref[...], weights_ref[...], 0.0)
    load_aux.wait()
    sums = dot(hi_lo_rows(lw), aux[...])
    sums = sums[0:1, :] + sums[1:2, :]
    for k in range(CHIPS):
        ssend[k] = sums[:, k * 128:(k + 1) * 128]
    srecv[g] = ssend[chip]
    for k in FAR_GRID:
        to = lax.rem(g + k, GRID)
        remote(ssend.at[to // 2], srecv.at[g], s_sem.at[0], s_sem.at[1], "grid", to)

    first, second = pairs_ref[0, 0], pairs_ref[0, 1]
    place = core * 256 + y * 128 + z * 16
    rows = pl.ds(pl.multiple_of(place, 16), 16)
    wait_bytes(facbuf.at[pl.ds(0, DIMERS - 1)], fa_sem.at[1])
    facsend[0] = facbuf[slot_ref[first]]
    facsend[1] = facbuf[slot_ref[second]]
    facall[:, rows, :] = facsend[...]
    for k in FAR_CHIPS:
        remote(
            facsend, facall.at[:, rows, :], fb_sem.at[0], fb_sem.at[1],
            "grid", 2 * lax.rem(chip + k, CHIPS) + core,
        )

    load_b.wait()
    for block in range(8):
        turned = b[:, block * 128:(block + 1) * 128].T
        for part in range(8):
            group = block * 8 + part
            half, owner = group // 32, group % 32
            place = half * 32 + (owner % 2) * 16 + ((owner // 2) % 2) * 8 + owner // 4
            bt[place * 16:(place + 1) * 16, :] = turned[part * 16:(part + 1) * 16, :]

    wait_bytes(facall.at[:, pl.ds(0, 240), :], fb_sem.at[1])
    own_half = pl.ds(pl.multiple_of(core * 256, 256), 256)
    remote(
        facall.at[:, own_half, :], facall.at[:, own_half, :], fc_sem.at[0], fc_sem.at[1],
        "grid", other_core,
    )

    def orbitals(half, of_core):
        rows = pl.ds(pl.multiple_of(of_core * 256, 256), 256)
        at = pl.ds(pl.multiple_of(half * FB + of_core * 256, 256), 256)
        turn = (((0,), (0,)), ((), ()))
        return lax.dot_general(
            facall[half, rows, :], bt[at, :], turn, preferred_element_type=F32
        )

    orb_first, orb_second = orbitals(0, core), orbitals(1, core)
    wait_bytes(facall.at[:, pl.ds(0, 256), :], fc_sem.at[1])
    orb_first += orbitals(0, 1 - core)
    orb_second += orbitals(1, 1 - core)
    density = jnp.sum(orb_first * orb_first + orb_second * orb_second, axis=0, keepdims=True)
    density = density * (1.0 / (2.0 * OCC))
    exchange = -EXCHANGE_COEFF * cube_root(density)

    parts = hi_lo_rows(lw * density)
    for part in range(2):
        fitted = dot(parts, aux[:, part * 1024:(part + 1) * 1024])
        fsend[part] = fitted[0:1, :] + fitted[1:2, :]
        frecv[chip, part] = fsend[part]
        for k in FAR_CHIPS:
            remote(
                fsend.at[part], frecv.at[chip, part], f_sem.at[0], f_sem.at[1],
                "grid", 2 * lax.rem(chip + k, CHIPS) + core,
            )
    for k in range(CHIPS):
        auxt[k * 128:(k + 1) * 128, :] = aux[:, k * 128:(k + 1) * 128].T

    local_exchange = jnp.sum(lw * exchange, axis=1, keepdims=True)
    local_weight = jnp.sum(lw, axis=1, keepdims=True)
    wait_bytes(srecv.at[pl.ds(0, GRID - 1)], s_sem.at[1])
    s_total = jnp.sum(srecv[...], axis=0)
    load_m.wait()
    wait_bytes(mbuf.at[0], m_sem.at[1])
    wait_bytes(frecv.at[pl.ds(0, CHIPS - 1)], f_sem.at[1])
    own_fitted = jnp.sum(frecv[...], axis=0)
    own_fitted = jnp.concatenate([own_fitted[0], own_fitted[1]], axis=1)

    rows_m = jnp.concatenate([mbuf[0], mbuf[1]], axis=0)
    terms = rows_m[:, 0:128] * own_fitted[:, 0:128]
    for k in range(1, CHIPS):
        cols = slice(k * 128, (k + 1) * 128)
        terms += rows_m[:, cols] * own_fitted[:, cols]
    coef_part = jnp.sum(terms.T, axis=0, keepdims=True)
    total_part = jnp.sum(coef_part * s_total, axis=1, keepdims=True) + local_exchange
    lane = lax.broadcasted_iota(jnp.int32, (1, 128), 1)
    csend[0:1, :] = coef_part
    csend[1:2, :] = jnp.where(lane == 0, total_part, jnp.where(lane == 1, local_weight, 0.0))
    crecv[g] = csend[...]
    for k in FAR_GRID:
        remote(
            csend, crecv.at[g], c_sem.at[0], c_sem.at[1], "grid", lax.rem(g + k, GRID)
        )
    wait_bytes(crecv.at[pl.ds(0, GRID - 1)], c_sem.at[1])

    totals = jnp.sum(crecv[...], axis=0)[1:2, :]
    average = totals[:, 0:1] / totals[:, 1:2]
    coefficients = jnp.concatenate(
        [crecv[2 * k, 0:1, :] + crecv[2 * k + 1, 0:1, :] for k in range(CHIPS)], axis=1
    )
    coulomb = dot(hi_lo_rows(coefficients), auxt[...])
    coulomb = coulomb[0:1, :] + coulomb[1:2, :]
    potential = lw * (coulomb + exchange - average)
    weighted = set()

    def product(chunk, other):
        half, column, _ = CHUNKS[chunk]
        of_core = 1 - core if other else core
        at = pl.ds(pl.multiple_of(half * FB + of_core * 256, 256), 256)
        if (half, other) not in weighted:
            weighted.add((half, other))
            wt[at, :] = (bt[at, :].astype(F32) * potential).astype(BF16)
        return dot(wt[at, :], b[:, column:column + NC])

    here = pl.ds(pl.multiple_of(y * 128, 128), 128)
    there = pl.ds(pl.multiple_of((1 - y) * 128, 128), 128)
    own_z = pl.ds(pl.multiple_of(z * 16, 16), 16)
    own_rows = pl.ds(pl.multiple_of(y * 128 + z * 16, 16), 16)
    there_rows = pl.ds(pl.multiple_of((1 - y) * 128 + z * 16, 16), 16)
    z_peers = [(k, lax.rem(z + k, 8)) for k in FAR_Z]

    def other_product(chunk):
        core_send[chunk] = product(chunk, True)
        remote(
            core_send.at[chunk], core_recv.at[chunk],
            core_sem.at[0, chunk], core_sem.at[1, chunk], "grid", other_core,
        )

    def own_product(chunk):
        acc[chunk] = product(chunk, False)

    def first_sum(chunk):
        wait_bytes(core_recv.at[chunk], core_sem.at[1, chunk])
        if CHUNKS[chunk][2] == "y":
            y_send[chunk] = (acc[chunk, there, :] + core_recv[chunk, there, :]).astype(BF16)
            remote(
                y_send.at[chunk], y_recv.at[chunk],
                y_sem.at[0, chunk], y_sem.at[1, chunk], "grid", other_y,
            )
            acc[chunk, here, :] += core_recv[chunk, here, :]
        else:
            acc[chunk] += core_recv[chunk]
            for line in range(2):
                for part in range(8):
                    row = line * 128 + part * 16
                    w_send[chunk, part, line] = acc[chunk, row:row + 16, :].astype(BF16)
            for k, to in z_peers:
                remote(
                    w_send.at[chunk, to], w_recv.at[chunk, k - 1],
                    z_sem.at[0, chunk], z_sem.at[1, chunk], "grid", to * 4 + y * 2 + core,
                )

    def second_sum(chunk):
        if CHUNKS[chunk][2] == "y":
            wait_bytes(y_recv.at[chunk], y_sem.at[1, chunk])
            acc[chunk, here, :] += y_recv[chunk].astype(F32)
            z_send[chunk] = acc[chunk, here, :].astype(BF16)
            for k, to in z_peers:
                at = pl.ds(pl.multiple_of(to * 16, 16), 16)
                remote(
                    z_send.at[chunk, at, :], z_recv.at[chunk, k - 1],
                    z_sem.at[0, chunk], z_sem.at[1, chunk], "grid", to * 4 + y * 2 + core,
                )
        else:
            wait_bytes(w_recv.at[chunk], z_sem.at[1, chunk])
            mine, theirs = acc[chunk, own_rows, :], acc[chunk, there_rows, :]
            for k in range(7):
                mine = mine + w_recv[chunk, k, y].astype(F32)
                theirs = theirs + w_recv[chunk, k, 1 - y].astype(F32)
            acc[chunk, own_rows, :] = mine
            v_send[chunk] = theirs.astype(BF16)
            remote(
                v_send.at[chunk], v_recv.at[chunk],
                y_sem.at[0, chunk], y_sem.at[1, chunk], "grid", other_y,
            )

    done = {}

    def ended(chunk):
        own = acc[chunk, own_rows, :]
        if CHUNKS[chunk][2] == "y":
            wait_bytes(z_recv.at[chunk], z_sem.at[1, chunk])
            for k in range(7):
                own = own + z_recv[chunk, k].astype(F32)
        else:
            wait_bytes(v_recv.at[chunk], y_sem.at[1, chunk])
            own = own + v_recv[chunk].astype(F32)
        done[chunk] = own

    steps = {"o": other_product, "w": own_product, "s": first_sum, "t": second_sum, "e": ended}
    for step in " ".join(SCHEDULE).split():
        steps[step[0]](int(step[1:]))

    def share(half, column):
        chunks = [i for i, c in enumerate(CHUNKS) if c[0] == half and c[1] // FB == column]
        for chunk in chunks:
            if chunk not in done:
                ended(chunk)
        return jnp.concatenate([done[i] for i in sorted(chunks, key=lambda i: CHUNKS[i][1])], axis=1)

    own_first, own_second = share(0, 0), share(1, 1)

    def for_fragment(index):
        return jnp.where(first == index, own_first, 0.0) + jnp.where(
            second == index, own_second, 0.0
        )

    for k in FAR_DIMERS:
        to = lax.rem(d + k, DIMERS)
        d_send[k - 1] = for_fragment(to)
        remote(
            d_send.at[k - 1], d_recv.at[k - 1], d_sem.at[0], d_sem.at[1], "dimer", to
        )
    own = for_fragment(d)
    out[1] = share(0, 1)
    wait_bytes(d_recv, d_sem.at[1])
    for k in range(DIMERS - 1):
        own = own + d_recv[k]
    out[0] = own

    wait_bytes(facbuf.at[pl.ds(0, DIMERS - 1)], fa_sem.at[0])
    wait_bytes(mbuf.at[0], m_sem.at[0])
    wait_bytes(facall.at[:, pl.ds(0, 240), :], fb_sem.at[0])
    wait_bytes(facall.at[:, pl.ds(0, 256), :], fc_sem.at[0])
    wait_bytes(srecv.at[pl.ds(0, GRID - 1)], s_sem.at[0])
    wait_bytes(frecv.at[pl.ds(0, CHIPS - 1)], f_sem.at[0])
    wait_bytes(crecv.at[pl.ds(0, GRID - 1)], c_sem.at[0])
    for chunk in range(len(CHUNKS)):
        y_first = CHUNKS[chunk][2] == "y"
        wait_bytes(core_recv.at[chunk], core_sem.at[0, chunk])
        wait_bytes((y_recv if y_first else v_recv).at[chunk], y_sem.at[0, chunk])
        wait_bytes((z_recv if y_first else w_recv).at[chunk], z_sem.at[0, chunk])
    wait_bytes(d_recv, d_sem.at[0])


def hand_out(both, frag_out, coup_out):
    frag_out[0] = both[0]
    coup_out[0] = both[1]


def shards(basis_values, aux_values, factors, frag_slot, dimer_pairs, counts, weights, metric_inv):
    vmem = pl.BlockSpec(memory_space=pltpu.VMEM)
    smem = pl.BlockSpec(memory_space=pltpu.SMEM)
    hbm = pl.BlockSpec(memory_space=pl.ANY)
    dma = pltpu.SemaphoreType.DMA
    n = len(CHUNKS)
    share = jax.ShapeDtypeStruct((1, FB // GRID, FB), F32)
    both = pl.pallas_call(
        kernel,
        name="fock",
        out_shape=jax.ShapeDtypeStruct((2, FB // GRID, FB), F32),
        in_specs=[hbm, hbm, vmem, smem, smem, vmem, vmem, hbm],
        out_specs=vmem,
        scratch_shapes=[
            pltpu.VMEM((PTS, 2 * FB), BF16),
            pltpu.VMEM((PTS, AUX), BF16),
            pltpu.VMEM((2 * FB, PTS), BF16),
            pltpu.VMEM((AUX, PTS), BF16),
            pltpu.VMEM((2 * FB, PTS), BF16),
            pltpu.VMEM((2, AUX // GRID, AUX), F32),
            pltpu.VMEM((DIMERS, FB // GRID, OCC), BF16),
            pltpu.VMEM((2, FB // GRID, OCC), BF16),
            pltpu.VMEM((2, FB, OCC), BF16),
            pltpu.VMEM((CHIPS, 1, 128), F32),
            pltpu.VMEM((GRID, 1, 128), F32),
            pltpu.VMEM((2, 1, AUX // 2), F32),
            pltpu.VMEM((CHIPS, 2, 1, AUX // 2), F32),
            pltpu.VMEM((2, 128), F32),
            pltpu.VMEM((GRID, 2, 128), F32),
            pltpu.VMEM((n, 256, NC), F32),
            pltpu.VMEM((n, 256, NC), F32),
            pltpu.VMEM((n, 256, NC), F32),
            pltpu.VMEM((n, 128, NC), BF16),
            pltpu.VMEM((n, 128, NC), BF16),
            pltpu.VMEM((n, 128, NC), BF16),
            pltpu.VMEM((n, 7, 16, NC), BF16),
            pltpu.VMEM((n, 8, 2, 16, NC), BF16),
            pltpu.VMEM((n, 7, 2, 16, NC), BF16),
            pltpu.VMEM((n, 16, NC), BF16),
            pltpu.VMEM((n, 16, NC), BF16),
            pltpu.VMEM((DIMERS - 1, 16, FB), F32),
            pltpu.VMEM((DIMERS - 1, 16, FB), F32),
            dma((3,)), dma((2,)), dma((2,)), dma((2,)), dma((2,)), dma((2,)), dma((2,)), dma((2,)),
            dma((2, n)), dma((2, n)), dma((2, n)), dma((2,)),
        ],
        compiler_params=pltpu.CompilerParams(
            collective_id=0, has_side_effects=True, vmem_limit_bytes=60 * 1024 * 1024
        ),
        cost_estimate=pl.CostEstimate(
            flops=2 * PTS * (2 * FB * OCC + 3 * AUX + 3 * FB * FB),
            bytes_accessed=2 * PTS * (2 * FB + AUX) + 4 * AUX * AUX // GRID,
            transcendentals=2 * PTS,
        ),
    )(basis_values, aux_values, factors, frag_slot, dimer_pairs, counts, weights, metric_inv)
    return pl.pallas_call(
        hand_out,
        name="outputs",
        out_shape=(share, share),
        in_specs=[vmem],
        out_specs=(vmem, vmem),
    )(both)


def solution(mesh):
    placed = (
        P("dimer", "grid", None),
        P("dimer", "grid", None),
        P("dimer", "grid", None),
        P(),
        P("dimer", None),
        P("dimer", "grid"),
        P("dimer", "grid"),
        P("dimer", "grid", None),
    )
    return jax.shard_map(
        shards,
        mesh=mesh,
        in_specs=placed,
        out_specs=(P("dimer", "grid", None), P("dimer", "grid", None)),
        check_vma=False,
    )
```

time: 63.6 us -> 56.9 us (0.89)
  Pallas kernels: 59.3 us -> 55.3 us
  local copies, waits for them, and re-layouts: 2.75 us -> 0 us
    pallas_call x1 -> x2, Pallas kernels: 59.3 us -> 55.3 us  [the longest x1 53.8 us: shards(): pl.pallas_call(kernel, name='fock', out_shape=jax.ShapeDtypeStruct((2, FB...]
    unnamed x2 -> x0, local copies, waits for them, and re-layouts: 2.75 us -> none
where the time goes in v2:
time: 56.9 us; the launch traced here: 56.6 us
  Pallas kernels  55.3 us (97%)
  between operations  1.29 us (2%)
    pallas_call x1, Pallas kernels, shards(): pl.pallas_call(kernel, name='fock', out_shape=jax.ShapeDtypeStruct((2, FB...  53.8 us
    pallas_call x1, Pallas kernels, shards(): pl.pallas_call(hand_out, name='outputs', out_shape=(share, share), in_spe...  1.47 us

profile of v2, /device:TPU:24, one launch (start us, length us, event | category | flops | bytes accessed | tf_op | source)
XLA Modules:
  0.0 56.6 jit_solution(5428168029906209227)
XLA Ops:
  1.3 53.8 %fock.1.both = f32[2,16,512]{2,1,0:T(8,128)} custom-call(bf16[1,1280,1024]{2,1,0:T(8,128)(2,1)} %basis_hbm.1, bf16[1,1280,2048]{2,1,0:T(8,128)(2,1)} %aux_hbm.1, bf16[1,16,128]{2,1,0:T(8,128)(2,1)} %fac_ref.1, s32[8]{0:T(128)} %slot_ref.1, s32[1,2]{1,0:T(1,128)} %pairs_ref.1, s32[1,1]{1,0:T(1,128)S(6)} %copy.10.counts_ref, f32[1,1280]{1,0:T(1,128)} %weights_ref.1, ...), custom_call_target="tpu_custom_call" | custom-call | flops 2364538880 | bytes 8388608 | tf_op jit(solution)/shard_map/fock/pallas_call | solution.py:365
  55.1 1.5 %outputs.1 = (f32[1,16,512]{2,1,0:T(8,128)}, f32[1,16,512]{2,1,0:T(8,128)}) custom-call(f32[2,16,512]{2,1,0:T(8,128)} %fock.1.both), custom_call_target="tpu_custom_call" | custom-call | tf_op jit(solution)/shard_map/outputs/pallas_call | solution.py:412

commit v3 on v2

--- a/solution.py
+++ b/solution.py
@@ -15,9 +15,13 @@
 FAR_CHIPS = sorted(range(1, 16), key=lambda k: -min(k, 16 - k))
 FAR_Z = sorted(range(1, 8), key=lambda k: -min(k, 8 - k))
 FAR_DIMERS = (2, 6, 4, 1, 3, 5, 7)
-NC = 256
 CHUNKS = (
-    (1, 768, "z"), (0, 0, "y"), (0, 256, "y"), (1, 512, "y"), (0, 512, "y"), (0, 768, "y"),
+    (1, 768, 256, "z"),
+    (0, 0, 256, "y"),
+    (0, 256, 256, "y"),
+    (1, 512, 256, "y"),
+    (0, 512, 256, "y"),
+    (0, 768, 256, "y"),
 )
 SCHEDULE = (
     "o0 w0 o1 w1", "o2 s0 w2 s1", "o3 w3 s2 o4", "w4 s3 o5 w5", "t1 s4 t2 s5",
@@ -69,9 +73,9 @@
 
 
 def kernel(
-    basis_hbm, aux_hbm, fac_ref, slot_ref, pairs_ref, counts_ref, weights_ref, metric_hbm,
+    basis_hbm, aux_hbm, fac_hbm, slot_hbm, pairs_hbm, counts_hbm, weights_hbm, metric_hbm,
     out,
-    b, aux, bt, auxt, wt, mbuf, facbuf, facsend, facall,
+    slot_ref, pairs_ref, counts_ref, weights_ref, b, aux, bt, auxt, wt, mbuf, facbuf, facsend, facall,
     ssend, srecv, fsend, frecv, csend, crecv,
     acc, core_send, core_recv, y_send, y_recv, z_send, z_recv,
     w_send, w_recv, v_send, v_recv, d_send, d_recv,
@@ -87,32 +91,41 @@
     other_core = g + 1 - 2 * core
     other_y = g + 2 - 4 * y
 
+    barrier = pltpu.get_barrier_semaphore()
+    for k in FAR_GRID:
+        pl.semaphore_signal(
+            barrier, inc=1, device_id={"grid": lax.rem(g + k, GRID)}, device_id_type=MESH
+        )
+    for k in FAR_DIMERS:
+        pl.semaphore_signal(
+            barrier, inc=1, device_id={"dimer": lax.rem(d + k, DIMERS)}, device_id_type=MESH
+        )
     load_b = pltpu.make_async_copy(basis_hbm.at[0], b, local_sem.at[0])
     load_aux = pltpu.make_async_copy(aux_hbm.at[0], aux, local_sem.at[1])
     load_m = pltpu.make_async_copy(metric_hbm.at[0], mbuf.at[core], local_sem.at[2])
     load_b.start()
     load_aux.start()
     load_m.start()
-
-    barrier = pltpu.get_barrier_semaphore()
-    for k in FAR_GRID:
-        pl.semaphore_signal(
-            barrier, inc=1, device_id={"grid": lax.rem(g + k, GRID)}, device_id_type=MESH
-        )
-    for k in FAR_DIMERS:
-        pl.semaphore_signal(
-            barrier, inc=1, device_id={"dimer": lax.rem(d + k, DIMERS)}, device_id_type=MESH
-        )
+    load_small = [
+        pltpu.make_async_copy(source, place, local_sem.at[3 + at])
+        for at, (source, place) in enumerate((
+            (slot_hbm, slot_ref), (pairs_hbm, pairs_ref), (counts_hbm, counts_ref),
+            (weights_hbm, weights_ref), (fac_hbm.at[0], facbuf.at[d]),
+        ))
+    ]
+    for load in load_small:
+        load.start()
     pl.semaphore_wait(barrier, GRID - 1 + DIMERS - 1)
 
     for k in FAR_DIMERS:
         remote(
-            fac_ref.at[0], facbuf.at[d], fa_sem.at[0], fa_sem.at[1],
+            fac_hbm.at[0], facbuf.at[d], fa_sem.at[0], fa_sem.at[1],
             "dimer", lax.rem(d + k, DIMERS),
         )
-    facbuf[d] = fac_ref[0]
     remote(metric_hbm.at[0], mbuf.at[core], m_sem.at[0], m_sem.at[1], "grid", other_core)
 
+    for load in load_small:
+        load.wait()
     position = lax.broadcasted_iota(jnp.int32, (1, PTS), 1)
     lw = jnp.where(position < counts_ref[...], weights_ref[...], 0.0)
     load_aux.wait()
@@ -171,13 +184,15 @@
     exchange = -EXCHANGE_COEFF * cube_root(density)
 
     parts = hi_lo_rows(lw * density)
-    for part in range(2):
-        fitted = dot(parts, aux[:, part * 1024:(part + 1) * 1024])
-        fsend[part] = fitted[0:1, :] + fitted[1:2, :]
-        frecv[chip, part] = fsend[part]
+    fitted = dot(parts, aux[...])
+    fitted = fitted[0:1, :] + fitted[1:2, :]
+    fsend[0] = fitted[:, 0:1024]
+    fsend[1] = fitted[:, 1024:2048]
+    frecv[chip] = fsend[...]
+    if True:
         for k in FAR_CHIPS:
             remote(
-                fsend.at[part], frecv.at[chip, part], f_sem.at[0], f_sem.at[1],
+                fsend, frecv.at[chip], f_sem.at[0], f_sem.at[1],
                 "grid", 2 * lax.rem(chip + k, CHIPS) + core,
             )
     for k in range(CHIPS):
@@ -221,13 +236,13 @@
     weighted = set()
 
     def product(chunk, other):
-        half, column, _ = CHUNKS[chunk]
+        half, column, wide, _ = CHUNKS[chunk]
         of_core = 1 - core if other else core
         at = pl.ds(pl.multiple_of(half * FB + of_core * 256, 256), 256)
         if (half, other) not in weighted:
             weighted.add((half, other))
             wt[at, :] = (bt[at, :].astype(F32) * potential).astype(BF16)
-        return dot(wt[at, :], b[:, column:column + NC])
+        return dot(wt[at, :], b[:, column:column + wide])
 
     here = pl.ds(pl.multiple_of(y * 128, 128), 128)
     there = pl.ds(pl.multiple_of((1 - y) * 128, 128), 128)
@@ -237,71 +252,71 @@
     z_peers = [(k, lax.rem(z + k, 8)) for k in FAR_Z]
 
     def other_product(chunk):
-        core_send[chunk] = product(chunk, True)
+        core_send[chunk][...] = product(chunk, True)
         remote(
-            core_send.at[chunk], core_recv.at[chunk],
+            core_send[chunk], core_recv[chunk],
             core_sem.at[0, chunk], core_sem.at[1, chunk], "grid", other_core,
         )
 
     def own_product(chunk):
-        acc[chunk] = product(chunk, False)
+        acc[chunk][...] = product(chunk, False)
 
     def first_sum(chunk):
-        wait_bytes(core_recv.at[chunk], core_sem.at[1, chunk])
-        if CHUNKS[chunk][2] == "y":
-            y_send[chunk] = (acc[chunk, there, :] + core_recv[chunk, there, :]).astype(BF16)
+        wait_bytes(core_recv[chunk], core_sem.at[1, chunk])
+        if CHUNKS[chunk][3] == "y":
+            y_send[chunk][...] = (acc[chunk][there, :] + core_recv[chunk][there, :]).astype(BF16)
             remote(
-                y_send.at[chunk], y_recv.at[chunk],
+                y_send[chunk], y_recv[chunk],
                 y_sem.at[0, chunk], y_sem.at[1, chunk], "grid", other_y,
             )
-            acc[chunk, here, :] += core_recv[chunk, here, :]
+            acc[chunk][here, :] += core_recv[chunk][here, :]
         else:
-            acc[chunk] += core_recv[chunk]
+            acc[chunk][...] += core_recv[chunk][...]
             for line in range(2):
                 for part in range(8):
                     row = line * 128 + part * 16
-                    w_send[chunk, part, line] = acc[chunk, row:row + 16, :].astype(BF16)
+                    w_send[chunk][part, line] = acc[chunk][row:row + 16, :].astype(BF16)
             for k, to in z_peers:
                 remote(
-                    w_send.at[chunk, to], w_recv.at[chunk, k - 1],
+                    w_send[chunk].at[to], w_recv[chunk].at[k - 1],
                     z_sem.at[0, chunk], z_sem.at[1, chunk], "grid", to * 4 + y * 2 + core,
                 )
 
     def second_sum(chunk):
-        if CHUNKS[chunk][2] == "y":
-            wait_bytes(y_recv.at[chunk], y_sem.at[1, chunk])
-            acc[chunk, here, :] += y_recv[chunk].astype(F32)
-            z_send[chunk] = acc[chunk, here, :].astype(BF16)
+        if CHUNKS[chunk][3] == "y":
+            wait_bytes(y_recv[chunk], y_sem.at[1, chunk])
+            acc[chunk][here, :] += y_recv[chunk][...].astype(F32)
+            z_send[chunk][...] = acc[chunk][here, :].astype(BF16)
             for k, to in z_peers:
                 at = pl.ds(pl.multiple_of(to * 16, 16), 16)
                 remote(
-                    z_send.at[chunk, at, :], z_recv.at[chunk, k - 1],
+                    z_send[chunk].at[at, :], z_recv[chunk].at[k - 1],
                     z_sem.at[0, chunk], z_sem.at[1, chunk], "grid", to * 4 + y * 2 + core,
                 )
         else:
-            wait_bytes(w_recv.at[chunk], z_sem.at[1, chunk])
-            mine, theirs = acc[chunk, own_rows, :], acc[chunk, there_rows, :]
+            wait_bytes(w_recv[chunk], z_sem.at[1, chunk])
+            mine, theirs = acc[chunk][own_rows, :], acc[chunk][there_rows, :]
             for k in range(7):
-                mine = mine + w_recv[chunk, k, y].astype(F32)
-                theirs = theirs + w_recv[chunk, k, 1 - y].astype(F32)
-            acc[chunk, own_rows, :] = mine
-            v_send[chunk] = theirs.astype(BF16)
+                mine = mine + w_recv[chunk][k, y].astype(F32)
+                theirs = theirs + w_recv[chunk][k, 1 - y].astype(F32)
+            acc[chunk][own_rows, :] = mine
+            v_send[chunk][...] = theirs.astype(BF16)
             remote(
-                v_send.at[chunk], v_recv.at[chunk],
+                v_send[chunk], v_recv[chunk],
                 y_sem.at[0, chunk], y_sem.at[1, chunk], "grid", other_y,
             )
 
     done = {}
 
     def ended(chunk):
-        own = acc[chunk, own_rows, :]
-        if CHUNKS[chunk][2] == "y":
-            wait_bytes(z_recv.at[chunk], z_sem.at[1, chunk])
+        own = acc[chunk][own_rows, :]
+        if CHUNKS[chunk][3] == "y":
+            wait_bytes(z_recv[chunk], z_sem.at[1, chunk])
             for k in range(7):
-                own = own + z_recv[chunk, k].astype(F32)
+                own = own + z_recv[chunk][k].astype(F32)
         else:
-            wait_bytes(v_recv.at[chunk], y_sem.at[1, chunk])
-            own = own + v_recv[chunk].astype(F32)
+            wait_bytes(v_recv[chunk], y_sem.at[1, chunk])
+            own = own + v_recv[chunk][...].astype(F32)
         done[chunk] = own
 
     steps = {"o": other_product, "w": own_product, "s": first_sum, "t": second_sum, "e": ended}
@@ -343,16 +358,11 @@
     wait_bytes(frecv.at[pl.ds(0, CHIPS - 1)], f_sem.at[0])
     wait_bytes(crecv.at[pl.ds(0, GRID - 1)], c_sem.at[0])
     for chunk in range(len(CHUNKS)):
-        y_first = CHUNKS[chunk][2] == "y"
-        wait_bytes(core_recv.at[chunk], core_sem.at[0, chunk])
-        wait_bytes((y_recv if y_first else v_recv).at[chunk], y_sem.at[0, chunk])
-        wait_bytes((z_recv if y_first else w_recv).at[chunk], z_sem.at[0, chunk])
+        y_first = CHUNKS[chunk][3] == "y"
+        wait_bytes(core_recv[chunk], core_sem.at[0, chunk])
+        wait_bytes((y_recv if y_first else v_recv)[chunk], y_sem.at[0, chunk])
+        wait_bytes((z_recv if y_first else w_recv)[chunk], z_sem.at[0, chunk])
     wait_bytes(d_recv, d_sem.at[0])
-
-
-def hand_out(both, frag_out, coup_out):
-    frag_out[0] = both[0]
-    coup_out[0] = both[1]
 
 
 def shards(basis_values, aux_values, factors, frag_slot, dimer_pairs, counts, weights, metric_inv):
@@ -361,14 +371,21 @@
     hbm = pl.BlockSpec(memory_space=pl.ANY)
     dma = pltpu.SemaphoreType.DMA
     n = len(CHUNKS)
-    share = jax.ShapeDtypeStruct((1, FB // GRID, FB), F32)
+
+    def per_chunk(shape, dtype):
+        return [pltpu.VMEM((*shape, chunk[2]), dtype) for chunk in CHUNKS]
+
     both = pl.pallas_call(
         kernel,
         name="fock",
-        out_shape=jax.ShapeDtypeStruct((2, FB // GRID, FB), F32),
-        in_specs=[hbm, hbm, vmem, smem, smem, vmem, vmem, hbm],
+        out_shape=pltpu.VMEM((2, FB // GRID, FB), F32),
+        in_specs=[hbm] * 8,
         out_specs=vmem,
         scratch_shapes=[
+            pltpu.SMEM((DIMERS,), jnp.int32),
+            pltpu.SMEM((1, 2), jnp.int32),
+            pltpu.VMEM((1, 1), jnp.int32),
+            pltpu.VMEM((1, PTS), F32),
             pltpu.VMEM((PTS, 2 * FB), BF16),
             pltpu.VMEM((PTS, AUX), BF16),
             pltpu.VMEM((2 * FB, PTS), BF16),
@@ -384,24 +401,24 @@
             pltpu.VMEM((CHIPS, 2, 1, AUX // 2), F32),
             pltpu.VMEM((2, 128), F32),
             pltpu.VMEM((GRID, 2, 128), F32),
-            pltpu.VMEM((n, 256, NC), F32),
-            pltpu.VMEM((n, 256, NC), F32),
-            pltpu.VMEM((n, 256, NC), F32),
-            pltpu.VMEM((n, 128, NC), BF16),
-            pltpu.VMEM((n, 128, NC), BF16),
-            pltpu.VMEM((n, 128, NC), BF16),
-            pltpu.VMEM((n, 7, 16, NC), BF16),
-            pltpu.VMEM((n, 8, 2, 16, NC), BF16),
-            pltpu.VMEM((n, 7, 2, 16, NC), BF16),
-            pltpu.VMEM((n, 16, NC), BF16),
-            pltpu.VMEM((n, 16, NC), BF16),
+            per_chunk((256,), F32),
+            per_chunk((256,), F32),
+            per_chunk((256,), F32),
+            per_chunk((128,), BF16),
+            per_chunk((128,), BF16),
+            per_chunk((128,), BF16),
+            per_chunk((7, 16), BF16),
+            per_chunk((8, 2, 16), BF16),
+            per_chunk((7, 2, 16), BF16),
+            per_chunk((16,), BF16),
+            per_chunk((16,), BF16),
             pltpu.VMEM((DIMERS - 1, 16, FB), F32),
             pltpu.VMEM((DIMERS - 1, 16, FB), F32),
-            dma((3,)), dma((2,)), dma((2,)), dma((2,)), dma((2,)), dma((2,)), dma((2,)), dma((2,)),
+            dma((8,)), dma((2,)), dma((2,)), dma((2,)), dma((2,)), dma((2,)), dma((2,)), dma((2,)),
             dma((2, n)), dma((2, n)), dma((2, n)), dma((2,)),
         ],
         compiler_params=pltpu.CompilerParams(
-            collective_id=0, has_side_effects=True, vmem_limit_bytes=60 * 1024 * 1024
+            collective_id=0, has_side_effects=True, vmem_limit_bytes=56 * 1024 * 1024
         ),
         cost_estimate=pl.CostEstimate(
             flops=2 * PTS * (2 * FB * OCC + 3 * AUX + 3 * FB * FB),
@@ -409,13 +426,7 @@
             transcendentals=2 * PTS,
         ),
     )(basis_values, aux_values, factors, frag_slot, dimer_pairs, counts, weights, metric_inv)
-    return pl.pallas_call(
-        hand_out,
-        name="outputs",
-        out_shape=(share, share),
-        in_specs=[vmem],
-        out_specs=(vmem, vmem),
-    )(both)
+    return both[0:1], both[1:2]
 
 
 def solution(mesh):

time: 56.9 us -> 55.1 us (0.968)
  Pallas kernels: 55.3 us -> 53 us
  local copies, waits for them, and re-layouts: 0 us -> 0.63 us
    pallas_call x2 -> x1, Pallas kernels: 55.3 us -> 53 us  [shards(): pl.pallas_call(kernel, name='fock', out_shape=pltpu.VMEM((2, FB // GRID,...]
    slice x0 -> x1, local copies, waits for them, and re-layouts: none -> 0.63 us  [shards(): return (both[0:1], both[1:2])]
where the time goes in v3:
time: 55.1 us; the launch traced here: 55 us
  Pallas kernels  53 us (96%)
  between operations  1.29 us (2%)
  local copies, waits for them, and re-layouts  0.63 us (1%)
    pallas_call x1, Pallas kernels, shards(): pl.pallas_call(kernel, name='fock', out_shape=pltpu.VMEM((2, FB // GRID,...  53 us

profile of v3, /device:TPU:24, one launch (start us, length us, event | category | flops | bytes accessed | tf_op | source)
XLA Modules:
  0.0 55.0 jit_solution(5215036339296300064)
XLA Ops:
  1.3 53.0 %fock.1 = f32[2,16,512]{2,1,0:T(8,128)S(1)} custom-call(bf16[1,1280,1024]{2,1,0:T(8,128)(2,1)} %basis_hbm.1, bf16[1,1280,2048]{2,1,0:T(8,128)(2,1)} %aux_hbm.1, bf16[1,16,128]{2,1,0:T(8,128)(2,1)} %fac_hbm.1, s32[8]{0:T(128)} %slot_hbm.1, s32[1,2]{1,0:T(1,128)} %pairs_hbm.1, s32[1,1]{1,0:T(1,128)S(6)} %copy.10.counts_hbm, f32[1,1280]{1,0:T(1,128)} %weights_hbm.1, ...), custom_call_target="tpu_custom_call" | custom-call | flops 2364538880 | bytes 8388608 | tf_op jit(solution)/shard_map/fock/pallas_call | solution.py:378
  54.3 0.6 %fusion = (f32[1,16,512]{2,1,0:T(8,128)}, f32[1,16,512]{2,1,0:T(8,128)}) fusion(f32[2,16,512]{2,1,0:T(8,128)S(1)} %fock.1), kind=kLoop, calls=%fused_computation | loop fusion | bytes 131072 | tf_op jit(solution)/shard_map/slice | solution.py:429
